TPU v7x, 32 devices: a whole 2x2x4 slice. The times are simulated.
32 devices in a mesh: dp: 2 (over x), depth: 2 (over y), tensor: 8 (over z, core).
Axes of the slice: x: 2, y: 2, z: 4, core: 2. Of those that a mesh axis runs over, the one named last changes fastest.
Arguments:
- text: bfloat16 [256, 8192], P(('dp', 'tensor')), may hold values from -6 to 6
- vision: bfloat16 [512, 8192], P(('dp', 'depth'), 'tensor'), may hold values from -6 to 6
- query_weight: bfloat16 [2, 8192, 2048], P('depth', None, 'tensor'), may hold values from -0.0625 to 0.0625
- key_weight: bfloat16 [2, 8192, 256], P('depth', 'tensor'), may hold values from -0.0625 to 0.0625
- value_weight: bfloat16 [2, 8192, 256], P('depth', 'tensor'), may hold values from -0.0625 to 0.0625
- out_weight: bfloat16 [2, 2048, 8192], P('depth', 'tensor'), may hold values from -0.25 to 0.25
- gate: float32 [2], P('depth'), may hold values from 0.5 to 1.5
- cotangent: bfloat16 [256, 8192], P(('dp', 'tensor')), may hold values from -0.75 to 0.75
- tile_table: int32 [2, 8, 4], P('dp'), may hold values 0 or 1
- vision_tiles: int32 [2], P('dp'), may hold values from 1 to 4
- text_lengths: int32 [2], P('dp'), may hold values from 64 to 128
Outputs:
- hidden_states: bfloat16 [2, 256, 8192], P('depth', ('dp', 'tensor'))
- text_grads: bfloat16 [2, 256, 8192], P('depth', ('dp', 'tensor'))
- vision_grad: float32 [512, 8192], P(('dp', 'depth'), 'tensor')
- key_weight_grad: float32 [2, 8192, 256], P('depth', 'tensor', 'dp')
- value_weight_grad: float32 [2, 8192, 256], P('depth', 'tensor', 'dp')
All inputs are finite; a program needn't handle non-finite values. No bound on the sum of `tile_table` on one device may be relied on, other than what follows from the above.
Results may differ from a plain program's by a relative error of at most 0.034.
Values may be sent and summed in bfloat16 or wider, within the bound.
A program may use at most 128 MiB of HBM per device.

v0:
```python
import math

import jax
import jax.numpy as jnp
from jax import lax
from jax.sharding import PartitionSpec as P

HD = 128
QGROUP = 8
SEQ = 128
TBLK = 16
TILES = 4
TILE_ROWS = 64
VIS = 256


def shifted(value, axis, steps):
    count = lax.axis_size(axis)
    first, last = (max(0, -steps), min(count, count - steps))
    return lax.ppermute(value, axis, [(source, source + steps) for source in range(first, last)])


def normalize(values, epsilon):
    return values * lax.rsqrt(jnp.mean(values * values, axis=-1, keepdims=True) + epsilon)


def norm_back(values, upstream, epsilon):
    inv_rms = lax.rsqrt(jnp.mean(values * values, axis=-1, keepdims=True) + epsilon)
    normed = values * inv_rms
    return inv_rms * (upstream - normed * jnp.mean(upstream * normed, axis=-1, keepdims=True))


def allowed_mask(table, tile_count, text_count):
    tile_ok = jnp.arange(TILES, dtype=jnp.int32) < tile_count
    block_ok = (table > 0) & tile_ok[None, :]
    full_mask = jnp.broadcast_to(
        block_ok[:, None, :, None], (SEQ // TBLK, TBLK, TILES, TILE_ROWS)
    ).reshape(SEQ, VIS)
    row_ok = jnp.arange(SEQ, dtype=jnp.int32) < text_count
    return full_mask & row_ok[:, None]


def token_rows(shard, transform):
    return transform(lax.all_gather(shard, "tensor", axis=0, tiled=True), jnp.int32(0))


def token_sums(term, shard_rows):
    return lax.psum_scatter(
        term(jnp.int32(0), shard_rows * lax.axis_size("tensor")).astype(jnp.bfloat16),
        "tensor",
        scatter_dimension=0,
        tiled=True,
    ).astype(jnp.float32)


def kv_totals(keys_part, values_part):
    return lax.psum((keys_part, values_part), "tensor")


def per_device(
    text,
    vision,
    query_weight,
    key_weight,
    value_weight,
    out_weight,
    gate,
    cotangent,
    tile_table,
    vision_tiles,
    text_lengths,
):
    layers = lax.axis_size("depth")
    section_index = lax.axis_index("depth")
    tensor_index = lax.axis_index("tensor")
    w_query = query_weight[0]
    w_key = key_weight[0]
    w_value = value_weight[0]
    w_out = out_weight[0]
    gate_value = jnp.tanh(gate[0])
    local_width = w_query.shape[1]
    local_heads = local_width // HD
    kv_width = w_key.shape[1]
    kv_heads = kv_width // HD
    shard_rows = text.shape[0]
    inv_sqrt = 1.0 / math.sqrt(HD)
    kv_group = tensor_index * local_heads // QGROUP
    allowed = allowed_mask(tile_table[0], vision_tiles[0], text_lengths[0])
    row_live = jnp.any(allowed, axis=-1).astype(jnp.float32)
    vis_full = lax.all_gather(vision, "depth", axis=0, tiled=True)
    keys_part = jnp.dot(vis_full, w_key, preferred_element_type=jnp.float32)
    values_part = jnp.dot(vis_full, w_value, preferred_element_type=jnp.float32)
    keys_pre, values_pre = kv_totals(keys_part, values_part)
    keys_cast = (
        normalize(keys_pre.reshape(VIS, kv_heads, HD), 1e-06)
        .astype(jnp.bfloat16)
        .reshape(VIS, kv_width)
    )
    values_cast = values_pre.astype(jnp.bfloat16)
    key_group = lax.dynamic_slice_in_dim(keys_cast, kv_group * HD, HD, 1)
    value_group = lax.dynamic_slice_in_dim(values_cast, kv_group * HD, HD, 1)
    current = text
    for layer_at in range(layers):

        def project(rows_in, offset):
            normed = normalize(rows_in.astype(jnp.float32), 1e-05).astype(jnp.bfloat16)
            return jnp.dot(normed, w_query, preferred_element_type=jnp.float32)

        layer_queries = token_rows(current, project).reshape(SEQ, local_heads, HD)
        layer_query_cast = normalize(layer_queries, 1e-06).astype(jnp.bfloat16)
        scores = (
            jnp.einsum(
                "shd,vd->hsv", layer_query_cast, key_group, preferred_element_type=jnp.float32
            )
            * inv_sqrt
        )
        expd = jnp.where(allowed[None], jnp.exp(scores), 0.0)
        layer_probs = expd / (
            jnp.sum(expd, axis=-1, keepdims=True) + (1.0 - row_live)[None, :, None]
        )
        layer_probs_cast = layer_probs.astype(jnp.bfloat16)
        mixed = jnp.einsum(
            "hsv,vd->shd", layer_probs_cast, value_group, preferred_element_type=jnp.float32
        )
        mixed_cast = mixed.astype(jnp.bfloat16).reshape(SEQ, local_width)

        def out_term(offset, number):
            return jnp.dot(mixed_cast, w_out, preferred_element_type=jnp.float32)

        attended = token_sums(out_term, shard_rows)
        outputs = (current.astype(jnp.float32) + gate_value * attended).astype(jnp.bfloat16)
        outputs, kept = (outputs, (layer_queries, layer_query_cast, layer_probs, layer_probs_cast))
        chosen = section_index == layer_at
        if layer_at == 0:
            saved_in, saved_out, saved_kept = (current, outputs, kept)
        else:
            saved_in = jnp.where(chosen, current, saved_in)
            saved_out = jnp.where(chosen, outputs, saved_out)
            saved_kept = jax.tree.map(
                lambda fresh, older: jnp.where(chosen, fresh, older), kept, saved_kept
            )
        if layer_at + 1 < layers:
            current = shifted(outputs, "depth", 1)
    upstream = cotangent
    for layer_at in reversed(range(layers)):
        queries, query_cast, probs, probs_cast = saved_kept
        scaled = (gate_value * upstream.astype(jnp.float32)).astype(jnp.bfloat16)

        def back_project(rows_in, offset):
            return jnp.einsum("sd,kd->sk", rows_in, w_out, preferred_element_type=jnp.float32)

        dmixed = token_rows(scaled, back_project).astype(jnp.bfloat16).reshape(SEQ, local_heads, HD)
        dprobs = jnp.einsum("shd,vd->hsv", dmixed, value_group, preferred_element_type=jnp.float32)
        layer_dvalues = jnp.einsum(
            "hsv,shd->vd", probs_cast, dmixed, preferred_element_type=jnp.float32
        )
        dscores = (
            probs * (dprobs - jnp.sum(probs * dprobs, axis=-1, keepdims=True)) * inv_sqrt
        ).astype(jnp.bfloat16)
        dquery_hat = jnp.einsum(
            "hsv,vd->shd", dscores, key_group, preferred_element_type=jnp.float32
        )
        layer_dkeys_hat = jnp.einsum(
            "hsv,shd->vd", dscores, query_cast, preferred_element_type=jnp.float32
        )
        dquery = (
            norm_back(queries, dquery_hat, 1e-06).astype(jnp.bfloat16).reshape(SEQ, local_width)
        )

        def in_term(offset, number):
            return jnp.einsum("sk,dk->sd", dquery, w_query, preferred_element_type=jnp.float32)

        dnormed = token_sums(in_term, shard_rows)
        dinputs = (
            upstream.astype(jnp.float32) + norm_back(saved_in.astype(jnp.float32), dnormed, 1e-05)
        ).astype(jnp.bfloat16)
        dinputs, kv_grads = (dinputs, (layer_dkeys_hat, layer_dvalues))
        chosen = section_index == layer_at
        if layer_at == layers - 1:
            saved_grad, saved_kv = (dinputs, kv_grads)
        else:
            saved_grad = jnp.where(chosen, dinputs, saved_grad)
            saved_kv = jax.tree.map(
                lambda fresh, older: jnp.where(chosen, fresh, older), kv_grads, saved_kv
            )
        if layer_at > 0:
            upstream = shifted(dinputs, "depth", -1)
    dkeys_hat, dvalues = saved_kv
    one_hot = (jnp.arange(kv_heads, dtype=jnp.int32) == kv_group).astype(jnp.float32)
    dkeys_full = (dkeys_hat[:, None, :] * one_hot[None, :, None]).reshape(VIS, kv_width)
    dvalues_full = (dvalues[:, None, :] * one_hot[None, :, None]).reshape(VIS, kv_width)
    dkeys_total, dvalues_total = kv_totals(dkeys_full, dvalues_full)
    dkeys_cast = (
        norm_back(
            keys_pre.reshape(VIS, kv_heads, HD), dkeys_total.reshape(VIS, kv_heads, HD), 1e-06
        )
        .astype(jnp.bfloat16)
        .reshape(VIS, kv_width)
    )
    dvalues_cast = dvalues_total.astype(jnp.bfloat16)
    dvision_part = jnp.einsum(
        "vc,dc->vd", dkeys_cast, w_key, preferred_element_type=jnp.float32
    ) + jnp.einsum("vc,dc->vd", dvalues_cast, w_value, preferred_element_type=jnp.float32)
    dvision = lax.psum_scatter(dvision_part, "depth", scatter_dimension=0, tiled=True)
    dkey_part = jnp.einsum("vd,vc->dc", vis_full, dkeys_cast, preferred_element_type=jnp.float32)
    dvalue_part = jnp.einsum(
        "vd,vc->dc", vis_full, dvalues_cast, preferred_element_type=jnp.float32
    )
    dkey_grad, dvalue_grad = (
        lax.psum_scatter(dkey_part, "dp", scatter_dimension=1, tiled=True),
        lax.psum_scatter(dvalue_part, "dp", scatter_dimension=1, tiled=True),
    )
    return (saved_out[None], saved_grad[None], dvision, dkey_grad[None], dvalue_grad[None])


def solution(mesh):
    in_specs = (
        P(("dp", "tensor"), None),
        P(("dp", "depth"), "tensor"),
        P("depth", None, "tensor"),
        P("depth", "tensor", None),
        P("depth", "tensor", None),
        P("depth", "tensor", None),
        P("depth"),
        P(("dp", "tensor"), None),
        P("dp", None, None),
        P("dp"),
        P("dp"),
    )
    out_specs = (
        P("depth", ("dp", "tensor"), None),
        P("depth", ("dp", "tensor"), None),
        P(("dp", "depth"), "tensor"),
        P("depth", "tensor", "dp"),
        P("depth", "tensor", "dp"),
    )
    return jax.shard_map(
        per_device, mesh=mesh, in_specs=in_specs, out_specs=out_specs, check_vma=False
    )
```

profile of v0, /device:TPU:0, one launch (start us, length us, event | category | flops | bytes accessed | tf_op | source)
XLA Modules:
  0.0 509.7 jit_solution(13643375281329998929)
XLA Ops:
  7.2 10.3 %all_gather.15 = bf16[256,1024]{1,0:T(8,128)(2,1)S(1)} all-gather(bf16[128,1024]{1,0:T(8,128)(2,1)} %param.12), channel_id=1, replica_groups=mesh['dp'=2,'depth'=2,'tensor'=8] {'depth'}, dimensions={0}, use_global_device_ids=true | all-gather | bytes 786432 | tf_op jit(solution)/shard_map/all_gather | solution.py:90
  19.4 6.4 %copy.74 = bf16[256,8192]{1,0:T(8,128)(2,1)} copy(bf16[256,8192]{0,1:T(8,128)(2,1)} %bitcast.172) | data formatting | bytes 8388608 | tf_op jit(solution)/shard_map/dot_general | solution.py:107
  27.9 2.5 and_reduce_fusion
  30.8 32.0 %all-reduce.8 = bf16[256,256]{1,0:T(8,128)(2,1)S(1)} all-reduce(f32[256,256]{1,0:T(8,128)S(1)} %fusion.66), channel_id=1, replica_groups=mesh['dp'=2,'depth'=2,'tensor'=8] {'tensor'}, use_global_device_ids=true, to_apply=%region_0.1 | all-reduce | flops 65536 | bytes 393216 | tf_op jit(solution)/shard_map/psum | solution.py:57
  62.8 12.6 %all-reduce.5.cloned.1.call-done = f32[256,256]{1,0:T(8,128)} async-done(((f32[256,256]{1,0:T(8,128)}), f32[256,256]{1,0:T(8,128)}) %all-reduce.5.cloned.1.call-update) | async-done | bytes 262160 | tf_op jit(solution)/shard_map/psum | solution.py:57
  75.4 1.1 reshape.236
  78.2 27.0 %all-gather.5.cloned.1.call-done = bf16[128,8192]{1,0:T(8,128)(2,1)} async-done(((bf16[16,8192]{1,0:T(8,128)(2,1)}), bf16[128,8192]{1,0:T(8,128)(2,1)}) %all-gather.5.cloned.1.call-update) | async-done | bytes 2097168 | tf_op jit(solution)/shard_map/all_gather | solution.py:44
  105.2 2.1 fusion.2
  107.3 4.3 multiply_reduce_fusion.8
  112.5 2.1 convolution_convert_fusion.3
  116.2 33.8 %reduce-scatter.8.cloned.1.call-done = bf16[16,8192]{1,0:T(8,128)(2,1)} async-done(((bf16[128,8192]{1,0:T(8,128)(2,1)}), bf16[16,8192]{1,0:T(8,128)(2,1)}) %reduce-scatter.8.cloned.1.call-update) | async-done | bytes 262160 | tf_op jit(solution)/shard_map/reduce_scatter | solution.py:48
  151.8 3.4 collective-permute-start
  155.2 3.9 collective-permute-done
  159.9 20.1 %all-gather.9.cloned.1.call-done = bf16[128,8192]{1,0:T(8,128)(2,1)} async-done(((bf16[16,8192]{1,0:T(8,128)(2,1)}), bf16[128,8192]{1,0:T(8,128)(2,1)}) %all-gather.9.cloned.1.call-update) | async-done | bytes 2097168 | tf_op jit(solution)/shard_map/all_gather | solution.py:44
  180.0 4.4 fusion.47
  185.2 25.5 %all-gather.7.cloned.1.call-done = bf16[128,8192]{1,0:T(8,128)(2,1)} async-done(((bf16[16,8192]{1,0:T(8,128)(2,1)}), bf16[128,8192]{1,0:T(8,128)(2,1)}) %all-gather.7.cloned.1.call-update) | async-done | bytes 2097168 | tf_op jit(solution)/shard_map/all_gather | solution.py:44
  210.7 2.1 fusion.4
  212.8 4.2 multiply_reduce_fusion.7
  217.8 1.4 multiply_reduce_fusion.5
  219.3 5.1 convolution_convert_fusion.1
  224.8 35.0 %reduce-scatter.12.cloned.1.call-done = bf16[16,8192]{1,0:T(8,128)(2,1)} async-done(((bf16[128,8192]{1,0:T(8,128)(2,1)}), bf16[16,8192]{1,0:T(8,128)(2,1)}) %reduce-scatter.12.cloned.1.call-update) | async-done | bytes 262160 | tf_op jit(solution)/shard_map/reduce_scatter | solution.py:48
  259.8 1.2 fusion.55
  261.1 1.2 fusion.53
  262.3 1.3 collective-permute-start.1
  263.6 7.0 %collective-permute-done.1 = bf16[16,8192]{1,0:T(8,128)(2,1)S(1)} collective-permute-done((bf16[16,8192]{1,0:T(8,128)(2,1)S(1)}, bf16[16,8192]{1,0:T(8,128)(2,1)S(1)}, u32[]{:S(2)}, u32[]{:S(2)}) %collective-permute-start.1) | collective-permute-done | bytes 262176 | tf_op jit(solution)/shard_map/ppermute | solution.py:20
  272.2 2.1 convolution_bitcast_fusion.6
  274.2 1.7 convolution_bitcast_fusion.4
  276.7 23.0 %all-gather.11.cloned.1.call-done = bf16[128,8192]{1,0:T(8,128)(2,1)} async-done(((bf16[16,8192]{1,0:T(8,128)(2,1)}), bf16[128,8192]{1,0:T(8,128)(2,1)}) %all-gather.11.cloned.1.call-update) | async-done | bytes 2097168 | tf_op jit(solution)/shard_map/all_gather | solution.py:44
  299.8 4.4 fusion.44
  305.2 1.5 fusion.42
  307.7 4.3 convolution_convert_fusion.2
  312.1 31.0 %all-reduce.9 = bf16[256,256]{1,0:T(8,128)(2,1)S(1)} all-reduce(f32[256,256]{1,0:T(8,128)S(1)} %get-tuple-element.22), channel_id=1, replica_groups=mesh['dp'=2,'depth'=2,'tensor'=8] {'tensor'}, use_global_device_ids=true, to_apply=%region_24.25 | all-reduce | flops 65536 | bytes 393216 | tf_op jit(solution)/shard_map/psum | solution.py:57
  343.2 1.3 convolution_bitcast_fusion
  344.5 18.1 %all-reduce.7.cloned.1.call-done = f32[256,256]{1,0:T(8,128)} async-done(((f32[256,256]{1,0:T(8,128)}), f32[256,256]{1,0:T(8,128)}) %all-reduce.7.cloned.1.call-update) | async-done | bytes 262160 | tf_op jit(solution)/shard_map/psum | solution.py:57
  365.8 1.3 convolution_bitcast_fusion.1
  367.2 1.5 multiply_reduce_fusion.4
  368.8 5.2 %convolution_convert_fusion = bf16[128,8192]{1,0:T(8,128)(2,1)} fusion(bf16[128,256]{0,1:T(8,128)(2,1)S(1)} %bitcast.182, bf16[1,8192,256]{2,1,0:T(8,128)(2,1)} %param.13), kind=kOutput, calls=%fused_computation.2 | convolution fusion | flops 537919488 | bytes 6356992 | tf_op jit(solution)/shard_map/sk,dk->sd/dot_general | solution.py:171
  374.0 25.7 %reduce-scatter.10.cloned.1.call-done = bf16[16,8192]{1,0:T(8,128)(2,1)} async-done(((bf16[128,8192]{1,0:T(8,128)(2,1)}), bf16[16,8192]{1,0:T(8,128)(2,1)}) %reduce-scatter.10.cloned.1.call-update) | async-done | bytes 262160 | tf_op jit(solution)/shard_map/reduce_scatter | solution.py:48
  399.7 1.8 fusion.77
  401.9 1.3 convolution_add_fusion
  403.2 17.5 %reduce-scatter.20.cloned.1.call-done = f32[1024,128]{0,1:T(8,128)} async-done(((f32[1024,256]{0,1:T(8,128)}), f32[1024,128]{0,1:T(8,128)}) %reduce-scatter.20.cloned.1.call-update) | async-done | bytes 524304 | tf_op jit(solution)/shard_map/reduce_scatter | solution.py:211
  420.7 2.0 copy.57
  422.7 20.6 %reduce-scatter.18.cloned.1.call-done = f32[1024,128]{0,1:T(8,128)} async-done(((f32[1024,256]{0,1:T(8,128)}), f32[1024,128]{0,1:T(8,128)}) %reduce-scatter.18.cloned.1.call-update) | async-done | bytes 524304 | tf_op jit(solution)/shard_map/reduce_scatter | solution.py:210
  443.4 2.0 copy.56
  445.4 35.9 %reduce-scatter.14.cloned.1.call-done = bf16[16,8192]{1,0:T(8,128)(2,1)} async-done(((bf16[128,8192]{1,0:T(8,128)(2,1)}), bf16[16,8192]{1,0:T(8,128)(2,1)}) %reduce-scatter.14.cloned.1.call-update) | async-done | bytes 262160 | tf_op jit(solution)/shard_map/reduce_scatter | solution.py:48
  481.3 1.2 fusion.59
  482.6 1.9 fusion.79
  484.5 18.7 %reduce-scatter.16.cloned.1.call-done = f32[128,1024]{1,0:T(8,128)} async-done(((f32[256,1024]{1,0:T(8,128)}), f32[128,1024]{1,0:T(8,128)}) %reduce-scatter.16.cloned.1.call-update) | async-done | bytes 524304 | tf_op jit(solution)/shard_map/reduce_scatter | solution.py:204
  (137 shorter events, 19.1 us)
Async XLA Ops:
  7.2 10.4 %copy-start = (bf16[1,1024,256]{2,1,0:T(8,128)(2,1)S(1)}, bf16[1,1024,256]{2,1,0:T(8,128)(2,1)}, u32[]{:S(2)}) copy-start(bf16[1,1024,256]{2,1,0:T(8,128)(2,1)} %param.14) | copy-start | bytes 1572868
  7.2 68.2 %all-reduce.5.cloned.1.call-start = ((), (), s32[]{:S(2)}) async-start(), calls=%async_computation.7 | async-start | bytes 524288 | tf_op jit(solution)/shard_map/psum | solution.py:57
  18.6 86.6 %all-gather.5.cloned.1.call-start = ((), (), s32[]{:S(2)}) async-start(), calls=%async_computation.8 | async-start | bytes 2359296 | tf_op jit(solution)/shard_map/all_gather | solution.py:44
  19.3 130.7 %reduce-scatter.8.cloned.1.call-start = ((), (), s32[]{:S(2)}) async-start(), calls=%async_computation.9 | async-start | bytes 2359296 | tf_op jit(solution)/shard_map/reduce_scatter | solution.py:48
  19.4 7.1 %copy-start.26 = (s32[1,8,4]{1,2,0:T(4,128)S(1)}, s32[1,8,4]{1,2,0:T(4,128)}, u32[]{:S(2)}) copy-start(s32[1,8,4]{1,2,0:T(4,128)} %param.19) | copy-start | bytes 388
  19.4 11.1 %copy-start.6 = (bf16[1,1024,256]{2,1,0:T(8,128)(2,1)S(1)}, bf16[1,1024,256]{2,1,0:T(8,128)(2,1)}, u32[]{:S(2)}) copy-start(bf16[1,1024,256]{2,1,0:T(8,128)(2,1)} %param.15) | copy-start | bytes 1572868
  27.9 83.8 %copy-start.24 = (pred[128,256]{0,1:T(8,128)(4,1)}, pred[128,256]{0,1:T(8,128)(4,1)S(1)}, u32[]{:S(2)}) copy-start(pred[128,256]{0,1:T(8,128)(4,1)S(1)} %copy.37) | copy-start | bytes 98308
  78.2 33.5 %copy-start.19 = (bf16[256,256]{1,0:T(8,128)(2,1)}, bf16[256,256]{1,0:T(8,128)(2,1)S(1)}, u32[]{:S(2)}) copy-start(bf16[256,256]{1,0:T(8,128)(2,1)S(1)} %bitcast_multiply_fusion.3) | copy-start | bytes 393220
  107.3 5.2 %copy-start.1 = (bf16[1,256,8192]{2,1,0:T(8,128)(2,1)S(1)}, bf16[1,256,8192]{2,1,0:T(8,128)(2,1)}, u32[]{:S(2)}) copy-start(bf16[1,256,8192]{2,1,0:T(8,128)(2,1)} %param.16) | copy-start | bytes 12582916
  111.6 0.7 copy-start.15
  111.7 0.8 copy-start.22
  112.5 2.9 copy-start.7
  112.5 37.5 %copy-start.4 = (bf16[16,8192]{1,0:T(8,128)(2,1)S(1)}, bf16[16,8192]{1,0:T(8,128)(2,1)}, u32[]{:S(2)}) copy-start(bf16[16,8192]{1,0:T(8,128)(2,1)} %param.11) | copy-start | bytes 786436
  114.6 65.3 %all-gather.9.cloned.1.call-start = ((), (), s32[]{:S(2)}) async-start(), calls=%async_computation.12 | async-start | bytes 2359296 | tf_op jit(solution)/shard_map/all_gather | solution.py:44
  116.2 94.6 %all-gather.7.cloned.1.call-start = ((), (), s32[]{:S(2)}) async-start(), calls=%async_computation.10 | async-start | bytes 2359296 | tf_op jit(solution)/shard_map/all_gather | solution.py:44
  151.1 0.7 copy-start.8
  151.8 7.3 %collective-permute-start = (bf16[16,8192]{1,0:T(8,128)(2,1)S(1)}, bf16[16,8192]{1,0:T(8,128)(2,1)S(1)}, u32[]{:S(2)}, u32[]{:S(2)}) collective-permute-start(bf16[16,8192]{1,0:T(8,128)(2,1)S(1)} %add_convert_fusion.1), channel_id=1, source_target_pairs={{0,8},{1,9},{2,10},{3,11},{4,12},{5,13},{6,14},{7,15},{16,24},{17,... | collective-permute-start | bytes 786440 | tf_op jit(solution)/shard_map/ppermute | solution.py:20
  159.1 0.7 copy-start.2
  159.8 100.0 %reduce-scatter.12.cloned.1.call-start = ((), (), s32[]{:S(2)}) async-start(), calls=%async_computation.13 | async-start | bytes 2359296 | tf_op jit(solution)/shard_map/reduce_scatter | solution.py:48
  184.3 32.7 %copy-start.14 = (bf16[16,2,8,128]{3,2,1,0:T(8,128)(2,1)}, bf16[16,2,8,128]{3,2,1,0:T(8,128)(2,1)S(1)}, u32[]{:S(2)}) copy-start(bf16[16,2,8,128]{3,2,1,0:T(8,128)(2,1)S(1)} %fusion.47) | copy-start | bytes 196612
  185.2 31.8 %copy-start.16 = (f32[128,2,128]{0,2,1:T(8,128)S(1)}, f32[128,2,128]{0,2,1:T(8,128)}, u32[]{:S(2)}) copy-start(f32[128,2,128]{0,2,1:T(8,128)} %copy-done.15) | copy-start | bytes 393220
  212.8 4.3 copy-start.20
  212.8 4.3 copy-start.25
  217.1 0.6 copy-start.23
  217.8 6.6 %copy-start.18 = (f32[2,128,256]{1,2,0:T(8,128)}, f32[2,128,256]{1,2,0:T(8,128)S(1)}, u32[]{:S(2)}) copy-start(f32[2,128,256]{1,2,0:T(8,128)S(1)} %get-tuple-element.19) | copy-start | bytes 786436
  219.2 5.4 %copy-start.3 = (bf16[16,8192]{1,0:T(8,128)(2,1)S(1)}, bf16[16,8192]{1,0:T(8,128)(2,1)}, u32[]{:S(2)}) copy-start(bf16[16,8192]{1,0:T(8,128)(2,1)} %copy-done.2) | copy-start | bytes 786436
  224.4 75.4 %all-gather.11.cloned.1.call-start = ((), (), s32[]{:S(2)}) async-start(), calls=%async_computation.14 | async-start | bytes 2359296 | tf_op jit(solution)/shard_map/all_gather | solution.py:44
  262.3 42.7 %copy-start.10 = (bf16[16,8192]{1,0:T(8,128)(2,1)}, bf16[16,8192]{1,0:T(8,128)(2,1)S(1)}, u32[]{:S(2)}) copy-start(bf16[16,8192]{1,0:T(8,128)(2,1)S(1)} %fusion.53) | copy-start | bytes 786436
  262.3 8.3 %collective-permute-start.1 = (bf16[16,8192]{1,0:T(8,128)(2,1)S(1)}, bf16[16,8192]{1,0:T(8,128)(2,1)S(1)}, u32[]{:S(2)}, u32[]{:S(2)}) collective-permute-start(bf16[16,8192]{1,0:T(8,128)(2,1)S(1)} %fusion.53), channel_id=1, source_target_pairs={{8,0},{9,1},{10,2},{11,3},{12,4},{13,5},{14,6},{15,7},{24,16},{25,... | collective-permute-start | bytes 786440 | tf_op jit(solution)/shard_map/ppermute | solution.py:20
  270.6 0.7 copy-start.12
  272.0 90.6 %all-reduce.7.cloned.1.call-start = ((), (), s32[]{:S(2)}) async-start(), calls=%async_computation.16 | async-start | bytes 524288 | tf_op jit(solution)/shard_map/psum | solution.py:57
  299.7 5.3 %copy-start.17 = (f32[256,128]{1,0:T(8,128)S(1)}, f32[256,128]{1,0:T(8,128)}, u32[]{:S(2)}) copy-start(f32[256,128]{1,0:T(8,128)} %convolution_bitcast_fusion.4) | copy-start | bytes 393220
  307.7 92.1 %reduce-scatter.10.cloned.1.call-start = ((), (), s32[]{:S(2)}) async-start(), calls=%async_computation.11 | async-start | bytes 2359296 | tf_op jit(solution)/shard_map/reduce_scatter | solution.py:48
  312.1 52.7 %copy-start.5 = (f32[256,256]{1,0:T(8,128)S(1)}, f32[256,256]{1,0:T(8,128)}, u32[]{:S(2)}) copy-start(f32[256,256]{1,0:T(8,128)} %all-reduce.5.cloned.1.call-done) | copy-start | bytes 786436
  312.1 108.6 %reduce-scatter.20.cloned.1.call-start = ((), (), s32[]{:S(2)}) async-start(), calls=%async_computation.19 | async-start | bytes 1572864 | tf_op jit(solution)/shard_map/reduce_scatter | solution.py:211
  344.5 98.9 %reduce-scatter.18.cloned.1.call-start = ((), (), s32[]{:S(2)}) async-start(), calls=%async_computation.18 | async-start | bytes 1572864 | tf_op jit(solution)/shard_map/reduce_scatter | solution.py:210
  364.4 2.8 copy-start.21
  367.2 114.2 %reduce-scatter.14.cloned.1.call-start = ((), (), s32[]{:S(2)}) async-start(), calls=%async_computation.15 | async-start | bytes 2359296 | tf_op jit(solution)/shard_map/reduce_scatter | solution.py:48
  368.7 31.0 %copy-start.9 = (bf16[16,8192]{1,0:T(8,128)(2,1)S(1)}, bf16[16,8192]{1,0:T(8,128)(2,1)}, u32[]{:S(2)}) copy-start(bf16[16,8192]{1,0:T(8,128)(2,1)} %copy-done.8) | copy-start | bytes 786436
  374.0 129.1 %reduce-scatter.16.cloned.1.call-start = ((), (), s32[]{:S(2)}) async-start(), calls=%async_computation.17 | async-start | bytes 1572864 | tf_op jit(solution)/shard_map/reduce_scatter | solution.py:204
  401.5 81.0 %copy-start.11 = (bf16[16,8192]{1,0:T(8,128)(2,1)S(1)}, bf16[16,8192]{1,0:T(8,128)(2,1)}, u32[]{:S(2)}) copy-start(bf16[16,8192]{1,0:T(8,128)(2,1)} %copy-done.10) | copy-start | bytes 786436
  401.5 81.0 %copy-start.13 = (bf16[16,8192]{1,0:T(8,128)(2,1)S(1)}, bf16[16,8192]{1,0:T(8,128)(2,1)}, u32[]{:S(2)}) copy-start(bf16[16,8192]{1,0:T(8,128)(2,1)} %copy-done.12) | copy-start | bytes 786436
Sparse Core Ops, SparseCore 0:
  18.7 56.6 all-reduce.4
  77.1 28.0 all-gather.4
  114.8 35.2 reduce-scatter.7
  152.2 27.7 all-gather.8
  182.1 28.5 all-gather.6
  224.5 35.3 reduce-scatter.11
  272.2 27.5 all-gather.10
  307.8 54.8 all-reduce.6
  365.0 34.7 reduce-scatter.9
  401.8 18.7 reduce-scatter.19
  423.0 20.3 reduce-scatter.17
  445.5 35.7 reduce-scatter.13
  484.1 18.9 reduce-scatter.15
where the time goes:
time: 511 us; the launch traced here: 510 us
  waiting for transfers between devices  325 us (64%)
  blocking collectives  73.3 us (14%)
  matrix products  51 us (10%)
  other arithmetic  21 us (4%)
  local copies, waits for them, and re-layouts  17.1 us (3%)
  between operations  16.5 us (3%)
  starting transfers between devices  5.45 us (1%)
    reduce_scatter x4, waiting for transfers between devices, token_sums(): lax.psum_scatter(term(jnp.int32(0), shard_rows * lax.axis_size('tensor'))...  130 us
    all_gather x4, waiting for transfers between devices, token_rows(): lax.all_gather(shard, 'tensor', axis=0, tiled=True)  95.6 us
    psum x2, blocking collectives, kv_totals(): return lax.psum((keys_part, values_part), 'tensor')  63 us
    psum x2, waiting for transfers between devices, kv_totals(): return lax.psum((keys_part, values_part), 'tensor')  30.7 us
    reduce_scatter x1, waiting for transfers between devices, per_device(): lax.psum_scatter(dkey_part, 'dp', scatter_dimension=1, tiled=True)  20.6 us
    reduce_scatter x1, waiting for transfers between devices, per_device(): lax.psum_scatter(dvision_part, 'depth', scatter_dimension=0, tiled=True)  18.7 us
    reduce_scatter x1, waiting for transfers between devices, per_device(): lax.psum_scatter(dvalue_part, 'dp', scatter_dimension=1, tiled=True)  17.5 us
    ppermute x2, waiting for transfers between devices, shifted(): lax.ppermute(value, axis, [(source, source + steps) for source in range(f...  10.8 us
  transfers between devices with their start and end apart: 15, of which 15 were waited for; matrix products, arithmetic and copies ran while one was open for 10% of the time, Pallas kernels for 0%

commit v1 on v0

--- a/solution.py
+++ b/solution.py
@@ -1,8 +1,11 @@
+import functools
 import math
 
 import jax
 import jax.numpy as jnp
 from jax import lax
+from jax.experimental import pallas as pl
+from jax.experimental.pallas import tpu as pltpu
 from jax.sharding import PartitionSpec as P
 
 HD = 128
@@ -12,6 +15,7 @@
 TILES = 4
 TILE_ROWS = 64
 VIS = 256
+CHUNKS = 4
 
 
 def shifted(value, axis, steps):
@@ -57,7 +61,7 @@
     return lax.psum((keys_part, values_part), "tensor")
 
 
-def per_device(
+def per_device_general(
     text,
     vision,
     query_weight,
@@ -213,6 +217,501 @@
     return (saved_out[None], saved_grad[None], dvision, dkey_grad[None], dvalue_grad[None])
 
 
+F32 = jnp.float32
+BF16 = jnp.bfloat16
+AG_AT = 0
+RS_AT = AG_AT + 2 * CHUNKS * 4
+HOP_AT = RS_AT + 2 * CHUNKS * 4
+KV_AT = HOP_AT + CHUNKS
+KVG_AT = KV_AT + 7
+DKR_AT = KVG_AT + 3
+DKA_AT = DKR_AT + 3
+VIS_AT = DKA_AT + 7
+VISX_AT = VIS_AT + 1
+DKX_AT = VIS_AT + 2
+DV_AT = VIS_AT + 3
+SEMS = VIS_AT + 4
+
+
+def dot_nn(a, b):
+    return lax.dot_general(a, b, (((1,), (0,)), ((), ())), preferred_element_type=F32)
+
+
+def dot_nt(a, b):
+    return lax.dot_general(a, b, (((1,), (1,)), ((), ())), preferred_element_type=F32)
+
+
+def dot_tn(a, b):
+    return lax.dot_general(a, b, (((0,), (0,)), ((), ())), preferred_element_type=F32)
+
+
+def layers_kernel(
+    text, vision, cot, wq_hbm, wk_hbm, wv_hbm, wo_hbm, gate, table, tile_count, text_count,
+    hid_out, grad_out, dvis_out, dkey_out, dvalue_out,
+    wq, wk, wv, wo, rows, term, pair, summed, arrived, hop_in, hop_out, acc_ref,
+    vis, vis_other, kv_part, kv_arrived, kv_all, key_pre, mask, qs, probs, mixed, dmixed, dq,
+    dk_part, dk_arrived, dk_all, dk_other, dvis_send, dvis_arrived, wsem, ssem, rsem,
+):
+    dp, depth, me = lax.axis_index("dp"), lax.axis_index("depth"), lax.axis_index("tensor")
+    z, core = me // 2, lax.rem(me, 2)
+    group, member = me // 4, lax.rem(me, 4)
+    width = text.shape[1]
+    step = width // CHUNKS
+    inv_sqrt = 1.0 / math.sqrt(HD)
+
+    def cols(k):
+        return pl.ds(k * step, step)
+
+    def remote(source, target, at, **device):
+        return pltpu.make_async_remote_copy(
+            src_ref=source, dst_ref=target, send_sem=ssem.at[at], recv_sem=rsem.at[at],
+            device_id=device, device_id_type=pl.DeviceIdType.MESH,
+        )
+
+    def at_z(offset):
+        return lax.rem(z + offset, 4) * 2 + core
+
+    def gather_z(slot, k, offset):
+        mine = rows.at[slot, core, z, :, cols(k)]
+        return remote(mine, mine, AG_AT + (slot * CHUNKS + k) * 4 + offset, tensor=at_z(offset))
+
+    def gather_pair(slot, k):
+        half = rows.at[slot, core, :, :, cols(k)]
+        return remote(half, half, AG_AT + (slot * CHUNKS + k) * 4, tensor=z * 2 + 1 - core)
+
+    def gather_start(slot, k):
+        for offset in (1, 2, 3):
+            gather_z(slot, k, offset).start()
+
+    def gather_turn(slot, k):
+        for offset in (1, 2, 3):
+            gather_z(slot, k, offset).wait_recv()
+        gather_pair(slot, k).start()
+
+    def gathered(slot, k):
+        gather_pair(slot, k).wait_recv()
+        return rows[slot, :, :, :, cols(k)].reshape(SEQ, step)
+
+    def sum_pair(slot, k):
+        return remote(
+            term.at[slot, 1 - core, :, cols(k)], pair.at[slot, :, cols(k)],
+            RS_AT + (slot * CHUNKS + k) * 4, tensor=z * 2 + 1 - core,
+        )
+
+    def sum_z(slot, k, offset):
+        return remote(
+            summed.at[slot, lax.rem(z + offset, 4), :, cols(k)],
+            arrived.at[slot, offset - 1, :, cols(k)],
+            RS_AT + (slot * CHUNKS + k) * 4 + offset, tensor=at_z(offset),
+        )
+
+    def sum_turn(slot, k):
+        sum_pair(slot, k).wait_recv()
+        total = term[slot, core, :, cols(k)].astype(F32) + pair[slot, :, cols(k)].astype(F32)
+        summed[slot, :, :, cols(k)] = total.astype(BF16).reshape(4, TBLK, step)
+        for offset in (1, 2, 3):
+            sum_z(slot, k, offset).start()
+
+    def sum_terms(slot, make):
+        for k in range(CHUNKS):
+            value = make(k).astype(BF16)
+            term[slot, 0, :, cols(k)] = value[: SEQ // 2]
+            term[slot, 1, :, cols(k)] = value[SEQ // 2 :]
+            sum_pair(slot, k).start()
+            if k > 0:
+                sum_turn(slot, k - 1)
+        sum_turn(slot, CHUNKS - 1)
+
+    def sum_result(slot, k):
+        for offset in (1, 2, 3):
+            sum_z(slot, k, offset).wait_recv()
+        total = summed[slot, z, :, cols(k)].astype(F32)
+        for offset in (1, 2, 3):
+            total += arrived[slot, offset - 1, :, cols(k)].astype(F32)
+        return total
+
+    def hop(k):
+        return remote(hop_out.at[:, cols(k)], hop_in.at[:, cols(k)], HOP_AT + k, depth=1 - depth)
+
+    def vis_copy():
+        return remote(vision, vis.at[depth], VIS_AT, depth=1 - depth)
+
+    def vis_other_copy():
+        return remote(vis, vis_other, VISX_AT, dp=1 - dp)
+
+    def kv_send(offset):
+        other = lax.rem(me + offset, 8)
+        return remote(
+            kv_part.at[other], kv_arrived.at[offset - 1], KV_AT + offset - 1, tensor=other
+        )
+
+    def in_group(offset):
+        return group * 4 + lax.rem(member + offset, 4)
+
+    def kv_share(offset):
+        return remote(
+            kv_all.at[member], kv_all.at[member], KVG_AT + offset - 1, tensor=in_group(offset)
+        )
+
+    def dk_send(offset):
+        return remote(
+            dk_part.at[lax.rem(member + offset, 4)], dk_arrived.at[offset - 1],
+            DKR_AT + offset - 1, tensor=in_group(offset),
+        )
+
+    def dk_share(offset):
+        return remote(
+            dk_all.at[me], dk_all.at[me], DKA_AT + offset - 1, tensor=lax.rem(me + offset, 8)
+        )
+
+    def dk_other_copy():
+        return remote(dk_all.at[pl.ds((1 - dp) * 4, 4)], dk_other, DKX_AT, dp=1 - dp)
+
+    def dvis_copy():
+        return remote(dvis_send, dvis_arrived, DV_AT, depth=1 - depth)
+
+    loads = [
+        pltpu.make_async_copy(source.at[0], target, wsem.at[at])
+        for at, (source, target) in enumerate(
+            ((wk_hbm, wk), (wv_hbm, wv), (wq_hbm, wq), (wo_hbm, wo))
+        )
+    ]
+    for load in loads:
+        load.start()
+    barrier = pltpu.get_barrier_semaphore()
+    for offset in range(1, 8):
+        pl.semaphore_signal(
+            barrier, inc=1, device_id={"tensor": lax.rem(me + offset, 8)},
+            device_id_type=pl.DeviceIdType.MESH,
+        )
+    pl.semaphore_signal(
+        barrier, inc=1, device_id={"depth": 1 - depth}, device_id_type=pl.DeviceIdType.MESH
+    )
+    pl.semaphore_signal(
+        barrier, inc=1, device_id={"dp": 1 - dp}, device_id_type=pl.DeviceIdType.MESH
+    )
+    pl.semaphore_wait(barrier, 9)
+
+    vis_copy().start()
+    for k in range(CHUNKS):
+        rows[0, core, z, :, cols(k)] = jnp.where(depth == 0, text[:, cols(k)], cot[:, cols(k)])
+        gather_start(0, k)
+    vis[depth] = vision[...]
+
+    lane_tile = lax.broadcasted_iota(jnp.int32, (TBLK, VIS), 1) // TILE_ROWS
+    row_at = lax.broadcasted_iota(jnp.int32, (TBLK, VIS), 0)
+    for block in range(SEQ // TBLK):
+        table_row = (block % 4) * 2 + block // 4
+        allowed = jnp.zeros((TBLK, VIS), F32)
+        for tile in range(TILES):
+            on = jnp.where((table[0, table_row, tile] > 0) & (tile < tile_count[0]), 1.0, 0.0)
+            allowed = jnp.where(lane_tile == tile, on, allowed)
+        allowed = jnp.where(row_at + table_row * TBLK < text_count[0], allowed, 0.0)
+        mask[pl.ds(block * TBLK, TBLK), :] = allowed
+    gate_value = jnp.tanh(jnp.full((TBLK, HD), gate[0], F32))[:, :1]
+    gate_rows = jnp.tanh(jnp.full((SEQ, HD), gate[0], F32))[:, :1]
+
+    vis_copy().wait_recv()
+    vis_other_copy().start()
+    loads[0].wait()
+    loads[1].wait()
+    states = vis[...].reshape(VIS, vision.shape[1])
+    keys = dot_nn(states, wk[...]).astype(BF16)
+    values = dot_nn(states, wv[...]).astype(BF16)
+    for owner in range(8):
+        here, head = pl.ds((owner % 4) * 64, 64), owner // 4
+        at = (owner % 4) * 64
+        kv_part[owner, :, :HD] = keys[at : at + 64, head * HD : (head + 1) * HD]
+        kv_part[owner, :, HD:] = values[at : at + 64, head * HD : (head + 1) * HD]
+    for offset in range(1, 8):
+        kv_send(offset).start()
+
+    def kv_reduce():
+        for offset in range(1, 8):
+            kv_send(offset).wait_recv()
+        total = kv_part[me].astype(F32)
+        for offset in range(1, 8):
+            total += kv_arrived[offset - 1].astype(F32)
+        pre = total[:, :HD]
+        key_pre[...] = pre
+        kv_all[member, :, :HD] = normalize(pre, 1e-06).astype(BF16)
+        kv_all[member, :, HD:] = total[:, HD:].astype(BF16)
+        for offset in (1, 2, 3):
+            kv_share(offset).start()
+
+    def project(slot, query, between=None):
+        total = jnp.zeros((SEQ, wq.shape[1]), F32)
+        squares = jnp.zeros((SEQ, 1), F32)
+        for k in range(CHUNKS):
+            block = gathered(slot, k)
+            if query:
+                total += dot_nn(block, wq[cols(k), :])
+                wide = block.astype(F32)
+                squares += jnp.sum(wide * wide, axis=-1, keepdims=True)
+            else:
+                total += dot_nt(block, wo[:, cols(k)])
+            if between is not None and k == CHUNKS // 2 - 1:
+                between()
+        if query:
+            return total * lax.rsqrt(squares * (1.0 / width) + 1e-05)
+        return (total * gate_rows).astype(BF16)
+
+    def heads():
+        return kv_all[:, :, :HD].reshape(VIS, HD), kv_all[:, :, HD:].reshape(VIS, HD)
+
+    def attend(query):
+        keys_cast, values_cast = heads()
+        allowed = mask[...]
+        dead = 1.0 - jnp.max(allowed, axis=-1, keepdims=True)
+        for head in range(2):
+            own = query[:, head * HD : (head + 1) * HD]
+            qs[head] = own
+            own_cast = normalize(own, 1e-06).astype(BF16)
+            expd = jnp.where(allowed > 0, jnp.exp(dot_nt(own_cast, keys_cast) * inv_sqrt), 0.0)
+            weights = expd / (jnp.sum(expd, axis=-1, keepdims=True) + dead)
+            probs[head] = weights
+            mixed[:, head * HD : (head + 1) * HD] = dot_nn(
+                weights.astype(BF16), values_cast
+            ).astype(BF16)
+
+    def attend_back():
+        keys_cast, values_cast = heads()
+        dkeys = jnp.zeros((VIS, HD), F32)
+        dvalues = jnp.zeros((VIS, HD), F32)
+        for head in range(2):
+            own, weights = qs[head], probs[head]
+            own_cast = normalize(own, 1e-06).astype(BF16)
+            upstream = dmixed[:, head * HD : (head + 1) * HD]
+            dprobs = dot_nt(upstream, values_cast)
+            dvalues += dot_tn(weights.astype(BF16), upstream)
+            dscores = (
+                weights
+                * (dprobs - jnp.sum(weights * dprobs, axis=-1, keepdims=True))
+                * inv_sqrt
+            ).astype(BF16)
+            dkeys += dot_tn(dscores, own_cast)
+            dq[:, head * HD : (head + 1) * HD] = norm_back(
+                own, dot_nn(dscores, keys_cast), 1e-06
+            ).astype(BF16)
+        dk_part[:, :, :HD] = dkeys.astype(BF16).reshape(4, 64, HD)
+        dk_part[:, :, HD:] = dvalues.astype(BF16).reshape(4, 64, HD)
+
+    def out_term(k):
+        return dot_nn(mixed[...], wo[:, cols(k)])
+
+    def in_term(k):
+        return dot_nt(dq[...], wq[cols(k), :])
+
+    def token_grad(slot, inputs, upstream):
+        squares = jnp.zeros((TBLK, 1), F32)
+        along = jnp.zeros((TBLK, 1), F32)
+        for k in range(CHUNKS):
+            dnormed = sum_result(slot, k)
+            acc_ref[:, cols(k)] = dnormed
+            wide = inputs[:, cols(k)].astype(F32)
+            squares += jnp.sum(wide * wide, axis=-1, keepdims=True)
+            along += jnp.sum(wide * dnormed, axis=-1, keepdims=True)
+        inv_rms = lax.rsqrt(squares * (1.0 / width) + 1e-05)
+        scale = along * (1.0 / width) * inv_rms * inv_rms
+        for k in range(CHUNKS):
+            wide = inputs[:, cols(k)].astype(F32)
+            grad_out[0, :, cols(k)] = (
+                upstream[:, cols(k)].astype(F32)
+                + inv_rms * (acc_ref[:, cols(k)] - wide * scale)
+            ).astype(BF16)
+
+    def layer_output(slot, k, inputs):
+        fresh = inputs[:, cols(k)].astype(F32) + gate_value * sum_result(slot, k)
+        hid_out[0, :, cols(k)] = fresh.astype(BF16)
+
+    def take_hop():
+        for k in range(CHUNKS):
+            hop(k).wait_recv()
+            rows[1, core, z, :, cols(k)] = hop_in[:, cols(k)]
+            gather_start(1, k)
+        for k in range(CHUNKS):
+            gather_turn(1, k)
+
+    def kv_ready():
+        for offset in (1, 2, 3):
+            kv_share(offset).wait_recv()
+
+    loads[2].wait()
+    loads[3].wait()
+    for k in range(CHUNKS):
+        gather_turn(0, k)
+    kv_reduce()
+
+    @pl.when(depth == 0)
+    def _():
+        query = project(0, True)
+        kv_ready()
+        attend(query)
+        sum_terms(0, out_term)
+        for k in range(CHUNKS):
+            layer_output(0, k, text)
+            hop_out[:, cols(k)] = hid_out[0, :, cols(k)]
+            hop(k).start()
+        take_hop()
+        dmixed[...] = project(1, False)
+        attend_back()
+        for offset in (1, 2, 3):
+            dk_send(offset).start()
+        sum_terms(1, in_term)
+
+    @pl.when(depth == 1)
+    def _():
+        dmixed[...] = project(0, False)
+        kv_ready()
+        take_hop()
+        attend(project(1, True))
+        attend_back()
+        sum_terms(0, in_term)
+        token_grad(0, hop_in, cot)
+        for k in range(CHUNKS):
+            hop_out[:, cols(k)] = grad_out[0, :, cols(k)]
+            hop(k).start()
+        for offset in (1, 2, 3):
+            dk_send(offset).start()
+        sum_terms(1, out_term)
+
+    for offset in (1, 2, 3):
+        dk_send(offset).wait_recv()
+    total = dk_part[member].astype(F32)
+    for offset in (1, 2, 3):
+        total += dk_arrived[offset - 1].astype(F32)
+    dk_all[me, :, :HD] = norm_back(key_pre[...], total[:, :HD], 1e-06).astype(BF16)
+    dk_all[me, :, HD:] = total[:, HD:].astype(BF16)
+    for offset in range(1, 8):
+        dk_share(offset).start()
+    for offset in range(1, 8):
+        dk_share(offset).wait_recv()
+    dk_other_copy().start()
+
+    def dvision(half):
+        first = dk_all[pl.ds(half * 2, 2)].reshape(VIS // 2, 2 * HD)
+        second = dk_all[pl.ds(4 + half * 2, 2)].reshape(VIS // 2, 2 * HD)
+        dkeys = jnp.concatenate([first[:, :HD], second[:, :HD]], axis=1)
+        dvalues = jnp.concatenate([first[:, HD:], second[:, HD:]], axis=1)
+        return dot_nt(dkeys, wk[...]) + dot_nt(dvalues, wv[...])
+
+    dvis_send[...] = dvision(1 - depth).astype(BF16)
+    dvis_copy().start()
+    dvis_out[...] = dvision(depth)
+    vis_other_copy().wait_recv()
+    grads = dot_tn(
+        vis[...].reshape(VIS, vision.shape[1]), dk_all[pl.ds(dp * 4, 4)].reshape(VIS, 2 * HD)
+    )
+    dk_other_copy().wait_recv()
+    grads += dot_tn(
+        vis_other[...].reshape(VIS, vision.shape[1]), dk_other[...].reshape(VIS, 2 * HD)
+    )
+    dkey_out[0] = grads[:, :HD]
+    dvalue_out[0] = grads[:, HD:]
+
+    @pl.when(depth == 0)
+    def _():
+        token_grad(1, text, hop_in)
+
+    @pl.when(depth == 1)
+    def _():
+        for k in range(CHUNKS):
+            layer_output(1, k, hop_in)
+
+    dvis_copy().wait_recv()
+    dvis_out[...] += dvis_arrived[...].astype(F32)
+
+    sent = [vis_copy(), vis_other_copy(), dk_other_copy(), dvis_copy()]
+    sent += [kv_send(offset) for offset in range(1, 8)]
+    sent += [dk_share(offset) for offset in range(1, 8)]
+    for offset in (1, 2, 3):
+        sent += [kv_share(offset), dk_send(offset)]
+    for k in range(CHUNKS):
+        sent.append(hop(k))
+        for slot in range(2):
+            sent += [gather_pair(slot, k), sum_pair(slot, k)]
+            for offset in (1, 2, 3):
+                sent += [gather_z(slot, k, offset), sum_z(slot, k, offset)]
+    for copy in sent:
+        copy.wait_send()
+
+
+def per_device(
+    text, vision, query_weight, key_weight, value_weight, out_weight, gate, cotangent,
+    tile_table, vision_tiles, text_lengths,
+):
+    n_dp, n_depth, n_tensor = (lax.axis_size(name) for name in ("dp", "depth", "tensor"))
+    shard, width = text.shape
+    features, kv_width = vision.shape[1], key_weight.shape[2]
+    local = query_weight.shape[2]
+    plain = (n_dp, n_depth, n_tensor, shard, local) == (2, 2, 8, TBLK, 2 * HD)
+    if not (plain and kv_width == 2 * HD and width % (CHUNKS * 2 * HD) == 0):
+        return per_device_general(
+            text, vision, query_weight, key_weight, value_weight, out_weight, gate, cotangent,
+            tile_table, vision_tiles, text_lengths,
+        )
+    vmem = pl.BlockSpec(memory_space=pltpu.VMEM)
+    smem = pl.BlockSpec(memory_space=pltpu.SMEM)
+    whole = pl.BlockSpec(memory_space=pl.ANY)
+    grad_columns = kv_width // n_dp
+    return pl.pallas_call(
+        layers_kernel,
+        out_shape=(
+            jax.ShapeDtypeStruct((1, shard, width), BF16),
+            jax.ShapeDtypeStruct((1, shard, width), BF16),
+            jax.ShapeDtypeStruct((VIS // 2, features), F32),
+            jax.ShapeDtypeStruct((1, features, grad_columns), F32),
+            jax.ShapeDtypeStruct((1, features, grad_columns), F32),
+        ),
+        in_specs=[vmem] * 3 + [whole] * 4 + [smem] * 4,
+        out_specs=(vmem,) * 5,
+        scratch_shapes=[
+            pltpu.VMEM((width, local), BF16),
+            pltpu.VMEM((features, kv_width), BF16),
+            pltpu.VMEM((features, kv_width), BF16),
+            pltpu.VMEM((local, width), BF16),
+            pltpu.VMEM((2, 2, 4, TBLK, width), BF16),
+            pltpu.VMEM((2, 2, SEQ // 2, width), BF16),
+            pltpu.VMEM((2, SEQ // 2, width), BF16),
+            pltpu.VMEM((2, 4, TBLK, width), BF16),
+            pltpu.VMEM((2, 3, TBLK, width), BF16),
+            pltpu.VMEM((TBLK, width), BF16),
+            pltpu.VMEM((TBLK, width), BF16),
+            pltpu.VMEM((TBLK, width), F32),
+            pltpu.VMEM((2, VIS // 2, features), BF16),
+            pltpu.VMEM((2, VIS // 2, features), BF16),
+            pltpu.VMEM((8, 64, 2 * HD), BF16),
+            pltpu.VMEM((7, 64, 2 * HD), BF16),
+            pltpu.VMEM((4, 64, 2 * HD), BF16),
+            pltpu.VMEM((64, HD), F32),
+            pltpu.VMEM((SEQ, VIS), F32),
+            pltpu.VMEM((2, SEQ, HD), F32),
+            pltpu.VMEM((2, SEQ, VIS), F32),
+            pltpu.VMEM((SEQ, local), BF16),
+            pltpu.VMEM((SEQ, local), BF16),
+            pltpu.VMEM((SEQ, local), BF16),
+            pltpu.VMEM((4, 64, 2 * HD), BF16),
+            pltpu.VMEM((3, 64, 2 * HD), BF16),
+            pltpu.VMEM((8, 64, 2 * HD), BF16),
+            pltpu.VMEM((4, 64, 2 * HD), BF16),
+            pltpu.VMEM((VIS // 2, features), BF16),
+            pltpu.VMEM((VIS // 2, features), BF16),
+            pltpu.SemaphoreType.DMA((4,)),
+            pltpu.SemaphoreType.DMA((SEMS,)),
+            pltpu.SemaphoreType.DMA((SEMS,)),
+        ],
+        compiler_params=pltpu.CompilerParams(
+            collective_id=0, has_side_effects=True, vmem_limit_bytes=52 * 1024 * 1024
+        ),
+        cost_estimate=pl.CostEstimate(
+            flops=6_000_000_000, bytes_accessed=16_000_000, transcendentals=100_000
+        ),
+    )(
+        text, vision, cotangent, query_weight, key_weight, value_weight, out_weight, gate,
+        tile_table, vision_tiles, text_lengths,
+    )
+
+
 def solution(mesh):
     in_specs = (
         P(("dp", "tensor"), None),

time: 511 us -> 190 us (0.37)
  waiting for transfers between devices: 325 us -> 0 us
  Pallas kernels: 0 us -> 177 us
  blocking collectives: 73.3 us -> 0 us
  matrix products: 51 us -> 0 us
  other arithmetic: 21 us -> 0 us
  between operations: 16.5 us -> 2.58 us
  local copies, waits for them, and re-layouts: 17.1 us -> 9.54 us
  starting transfers between devices: 5.45 us -> 0 us
    reduce_scatter x7 -> x0, waiting for transfers between devices: 187 us -> none  [the longest x4 130 us: token_sums(): lax.psum_scatter(term(jnp.int32(0), shard_rows * lax.axis_size('tensor'))...]
    pallas_call x0 -> x1, Pallas kernels: none -> 177 us  [per_device(): pl.pallas_call(layers_kernel, out_shape=(jax.ShapeDtypeStruct((1, shard,...]
    all_gather x4 -> x0, waiting for transfers between devices: 95.6 us -> none  [token_rows(): lax.all_gather(shard, 'tensor', axis=0, tiled=True)]
    psum x2 -> x0, blocking collectives: 63 us -> none  [kv_totals(): return lax.psum((keys_part, values_part), 'tensor')]
    dot_general x26 -> x0, matrix products: 51 us -> none  [the longest x2 10.3 us: in_term(): jnp.einsum('sk,dk->sd', dquery, w_query, preferred_element_type=jnp.float32)]
    psum x2 -> x0, waiting for transfers between devices: 30.7 us -> none  [kv_totals(): return lax.psum((keys_part, values_part), 'tensor')]
    ppermute x2 -> x0, waiting for transfers between devices: 10.8 us -> none  [shifted(): lax.ppermute(value, axis, [(source, source + steps) for source in range(f...]
    all_gather x1 -> x0, blocking collectives: 10.3 us -> none  [per_device(): vis_full = lax.all_gather(vision, 'depth', axis=0, tiled=True)]
  transfers between devices with their start and end apart: 15 -> 0, of which waited for: 15 -> 0; matrix products, arithmetic and copies ran while one was open for 10% -> 0% of each run, Pallas kernels for 0% -> 0%
where the time goes in v1:
time: 190 us; the launch traced here: 189 us
  Pallas kernels  177 us (93%)
  local copies, waits for them, and re-layouts  9.54 us (5%)
  between operations  2.58 us (1%)
    pallas_call x1, Pallas kernels, per_device(): pl.pallas_call(layers_kernel, out_shape=(jax.ShapeDtypeStruct((1, shard,...  177 us
    unnamed x12, local copies, waits for them, and re-layouts  9.54 us

profile of v1, /device:TPU:0, one launch (start us, length us, event | category | flops | bytes accessed | tf_op | source)
XLA Modules:
  0.0 189.3 jit_solution(5922062472674716073)
XLA Ops:
  2.6 0.8 copy.16.table
  3.3 0.0 copy-start
  3.3 0.9 copy-done
  4.3 0.0 copy-start.1
  4.3 0.9 copy-done.1
  5.2 0.0 copy-start.2
  5.2 0.9 copy-done.2
  6.2 177.1 %shard_map.146 = (bf16[1,16,8192]{2,1,0:T(8,128)(2,1)S(1)}, bf16[1,16,8192]{2,1,0:T(8,128)(2,1)S(1)}, f32[128,1024]{1,0:T(8,128)S(1)}, f32[1,1024,128]{2,1,0:T(8,128)}, f32[1,1024,128]{2,1,0:T(8,128)}) custom-call(bf16[16,8192]{1,0:T(8,128)(2,1)S(1)} %copy-done, bf16[128,1024]{1,0:T(8,128)(2,1)S(1)} %copy-done.1, bf16[16,8192]{1,0:T(8,128)(2,1)S(1)} %copy-done.2, ...), custom_call_target="tpu_custom_call" | custom-call | flops 6000000000 | bytes 16000000 | tf_op jit(solution)/shard_map/pallas_call | solution.py:657
  183.3 0.7 copy.25
  184.0 0.7 copy.26
  184.7 0.8 copy.27
  185.5 1.9 copy.28
  187.4 1.9 copy.29
Async XLA Ops:
  3.3 0.9 copy-start
  4.3 0.9 copy-start.1
  5.2 0.9 copy-start.2

commit v2 on v1

--- a/solution.py
+++ b/solution.py
@@ -220,7 +220,7 @@
 F32 = jnp.float32
 BF16 = jnp.bfloat16
 AG_AT = 0
-RS_AT = AG_AT + 2 * CHUNKS * 4
+RS_AT = AG_AT + 2 * CHUNKS * 6
 HOP_AT = RS_AT + 2 * CHUNKS * 4
 KV_AT = HOP_AT + CHUNKS
 KVG_AT = KV_AT + 7
@@ -271,22 +271,75 @@
     def at_z(offset):
         return lax.rem(z + offset, 4) * 2 + core
 
-    def gather_z(slot, k, offset):
-        mine = rows.at[slot, core, z, :, cols(k)]
-        return remote(mine, mine, AG_AT + (slot * CHUNKS + k) * 4 + offset, tensor=at_z(offset))
+    def gather_z(slot, k, source, target, send_at):
+        block = rows.at[slot, core, source, :, cols(k)]
+        base = AG_AT + (slot * CHUNKS + k) * 6
+        return pltpu.make_async_remote_copy(
+            src_ref=block, dst_ref=block, send_sem=ssem.at[base + send_at],
+            recv_sem=rsem.at[base + 1 + source], device_id={"tensor": target * 2 + core},
+            device_id_type=pl.DeviceIdType.MESH,
+        )
+
+    def gather_up(slot, k, source):
+        return gather_z(slot, k, source, lax.rem(z + 1, 4), 1 + source)
+
+    def gather_down(slot, k, source, send_at):
+        return gather_z(slot, k, source, lax.rem(z + 3, 4), send_at)
 
     def gather_pair(slot, k):
         half = rows.at[slot, core, :, :, cols(k)]
-        return remote(half, half, AG_AT + (slot * CHUNKS + k) * 4, tensor=z * 2 + 1 - core)
+        return remote(half, half, AG_AT + (slot * CHUNKS + k) * 6, tensor=z * 2 + 1 - core)
 
     def gather_start(slot, k):
-        for offset in (1, 2, 3):
-            gather_z(slot, k, offset).start()
+        @pl.when(z < 3)
+        def _():
+            gather_up(slot, k, z).start()
+
+        @pl.when(z > 0)
+        def _():
+            gather_down(slot, k, z, 5).start()
+
+    def gather_pass(slot, k, far):
+        @pl.when(z >= far)
+        def _():
+            gather_up(slot, k, z - far).wait_recv()
+
+            @pl.when(z < 3)
+            def _():
+                gather_up(slot, k, z - far).start()
+
+        @pl.when(z + far <= 3)
+        def _():
+            gather_down(slot, k, z + far, 1 + z + far).wait_recv()
+
+            @pl.when(z > 0)
+            def _():
+                gather_down(slot, k, z + far, 1 + z + far).start()
 
     def gather_turn(slot, k):
-        for offset in (1, 2, 3):
-            gather_z(slot, k, offset).wait_recv()
+        gather_pass(slot, k, 3)
         gather_pair(slot, k).start()
+
+    def gather_sent(slot, k):
+        gather_pair(slot, k).wait_send()
+
+        @pl.when(z < 3)
+        def _():
+            gather_up(slot, k, z).wait_send()
+
+        @pl.when(z > 0)
+        def _():
+            gather_down(slot, k, z, 5).wait_send()
+
+        for far in (1, 2, 3):
+
+            @pl.when((z >= far) & (z < 3))
+            def _():
+                gather_up(slot, k, z - far).wait_send()
+
+            @pl.when((z + far <= 3) & (z > 0))
+            def _():
+                gather_down(slot, k, z + far, 1 + z + far).wait_send()
 
     def gathered(slot, k):
         gather_pair(slot, k).wait_recv()
@@ -439,10 +492,13 @@
         for offset in (1, 2, 3):
             kv_share(offset).start()
 
-    def project(slot, query, between=None):
+    def project(slot, query):
         total = jnp.zeros((SEQ, wq.shape[1]), F32)
         squares = jnp.zeros((SEQ, 1), F32)
-        for k in range(CHUNKS):
+        gather_turn(slot, 0)
+        for k in range(CHUNKS):
+            if k + 1 < CHUNKS:
+                gather_turn(slot, k + 1)
             block = gathered(slot, k)
             if query:
                 total += dot_nn(block, wq[cols(k), :])
@@ -450,8 +506,6 @@
                 squares += jnp.sum(wide * wide, axis=-1, keepdims=True)
             else:
                 total += dot_nt(block, wo[:, cols(k)])
-            if between is not None and k == CHUNKS // 2 - 1:
-                between()
         if query:
             return total * lax.rsqrt(squares * (1.0 / width) + 1e-05)
         return (total * gate_rows).astype(BF16)
@@ -529,8 +583,11 @@
             hop(k).wait_recv()
             rows[1, core, z, :, cols(k)] = hop_in[:, cols(k)]
             gather_start(1, k)
-        for k in range(CHUNKS):
-            gather_turn(1, k)
+            if k > 0:
+                gather_pass(1, k - 1, 1)
+        gather_pass(1, CHUNKS - 1, 1)
+        for k in range(CHUNKS):
+            gather_pass(1, k, 2)
 
     def kv_ready():
         for offset in (1, 2, 3):
@@ -538,8 +595,9 @@
 
     loads[2].wait()
     loads[3].wait()
-    for k in range(CHUNKS):
-        gather_turn(0, k)
+    for far in (1, 2):
+        for k in range(CHUNKS):
+            gather_pass(0, k, far)
     kv_reduce()
 
     @pl.when(depth == 0)
@@ -629,9 +687,10 @@
     for k in range(CHUNKS):
         sent.append(hop(k))
         for slot in range(2):
-            sent += [gather_pair(slot, k), sum_pair(slot, k)]
+            gather_sent(slot, k)
+            sent.append(sum_pair(slot, k))
             for offset in (1, 2, 3):
-                sent += [gather_z(slot, k, offset), sum_z(slot, k, offset)]
+                sent.append(sum_z(slot, k, offset))
     for copy in sent:
         copy.wait_send()
 

time: 190 us -> 175 us (0.921)
  Pallas kernels: 177 us -> 163 us
    pallas_call x1, Pallas kernels: 177 us -> 163 us  [per_device(): pl.pallas_call(layers_kernel, out_shape=(jax.ShapeDtypeStruct((1, shard,...]
where the time goes in v2:
time: 175 us
  Pallas kernels  163 us (93%)
  local copies, waits for them, and re-layouts  9.54 us (5%)
  between operations  2.58 us (1%)
    pallas_call x1, Pallas kernels, per_device(): pl.pallas_call(layers_kernel, out_shape=(jax.ShapeDtypeStruct((1, shard,...  163 us
    unnamed x12, local copies, waits for them, and re-layouts  9.54 us

profile of v2, /device:TPU:0, one launch (start us, length us, event | category | flops | bytes accessed | tf_op | source)
XLA Modules:
  0.0 174.7 jit_solution(8587086374291922736)
XLA Ops:
  2.6 0.8 copy.16.table
  3.3 0.0 copy-start
  3.3 0.9 copy-done
  4.3 0.0 copy-start.1
  4.3 0.9 copy-done.1
  5.2 0.0 copy-start.2
  5.2 0.9 copy-done.2
  6.2 162.5 %shard_map.146 = (bf16[1,16,8192]{2,1,0:T(8,128)(2,1)S(1)}, bf16[1,16,8192]{2,1,0:T(8,128)(2,1)S(1)}, f32[128,1024]{1,0:T(8,128)S(1)}, f32[1,1024,128]{2,1,0:T(8,128)}, f32[1,1024,128]{2,1,0:T(8,128)}) custom-call(bf16[16,8192]{1,0:T(8,128)(2,1)S(1)} %copy-done, bf16[128,1024]{1,0:T(8,128)(2,1)S(1)} %copy-done.1, bf16[16,8192]{1,0:T(8,128)(2,1)S(1)} %copy-done.2, ...), custom_call_target="tpu_custom_call" | custom-call | flops 6000000000 | bytes 16000000 | tf_op jit(solution)/shard_map/pallas_call | solution.py:716
  168.7 0.7 copy.25
  169.4 0.7 copy.26
  170.1 0.8 copy.27
  170.9 1.9 %copy.28 = f32[1,1024,128]{2,1,0:T(8,128)} copy(f32[1,1024,128]{2,1,0:T(8,128)} %get-tuple-element.13) | data formatting | bytes 1048576
  172.8 1.9 %copy.29 = f32[1,1024,128]{2,1,0:T(8,128)} copy(f32[1,1024,128]{2,1,0:T(8,128)} %get-tuple-element.14) | data formatting | bytes 1048576
Async XLA Ops:
  3.3 0.9 copy-start
  4.3 0.9 copy-start.1
  5.2 0.9 copy-start.2
